TPU v7x, 512 devices: a whole 4x4x16 slice. The times are simulated.
512 devices in a mesh: dp: 64 (over y_lo, z, core), mp: 8 (over x, y_hi).
Axes of the slice: x: 4, y: 4 (y_hi: 2, y_lo: 2; y = y_hi * 2 + y_lo), z: 16, core: 2. Of those that a mesh axis runs over, the one named last changes fastest.
Arguments:
- tokens: bfloat16 [16384, 4096], P('dp'), may hold values from -6 to 6
- hidden_grad: bfloat16 [16384, 8192], P('dp', 'mp'), may hold values from -6 to 6
- w_in: bfloat16 [4096, 8192], P('dp', 'mp'), may hold values from -0.09375 to 0.09375
- b_in: float32 [8192], P('mp'), may hold values from -4 to 4
- query_in: bfloat16 [2048, 4096], P('dp'), may hold values from -0.09375 to 0.09375
- query_hidden: bfloat16 [2048, 8192], P('dp', 'mp'), may hold values from -0.015625 to 0.015625
- owners: int32 [64], replicated, may hold values from 0 to 63, each once
- routes: int32 [16384, 1], P('dp'), may hold values from 0 to 63; in each aligned block of 256 rows (0 to 255, 256 to 511, ...) at most 8 rows name the same one
- example_slot: int32 [16384], P('dp'), may hold values from 0 to 7
Outputs:
- scores: float32 [512, 16], P('dp')
Inputs may be any that keep to these rules, and one draw needn't show every extreme that they name: A permutation; batch b's factors are in slot owners[b]. `routes`: among the 256 tokens of one index of dp, no destination is named more than 8 times, a bound that some block reaches.
All inputs are finite; a program needn't handle non-finite values.
Results may differ from a plain program's by a relative error of at most 0.0003.
Values may be sent and summed in bfloat16 or wider, within the bound.
A program may use at most 64 MiB of HBM per device.

v0:
```python
import jax
import jax.numpy as jnp
from jax import lax
from jax.sharding import PartitionSpec as P

EX_OUT = 8
QB = 4
RANK = 8
NB = 4


def spread(value, axis, source):
    kept = jnp.where(lax.axis_index(axis) == source, value, 0).astype(value.dtype)
    return lax.psum(kept, axis)


def slope(pre):
    cdf = 0.5 * (1.0 + jax.scipy.special.erf(pre * 0.7071067811865476))
    dens = jnp.exp(-0.5 * pre * pre) * 0.3989422804014327
    return cdf + pre * dens


def body(tokens, hidden_grad, w_in, b_in, query_in, query_hidden, owners, routes, example_slot):
    n_dp = lax.axis_size("dp")
    lefts = []
    rights = []
    for batch in range(NB):
        root = owners[batch]
        left_f, right_f = (spread(query_in, "dp", root), spread(query_hidden, "dp", root))
        lefts.append(left_f)
        rights.append(right_f)
    factors_in = jnp.concatenate(lefts, axis=0)
    factors_hidden = jnp.concatenate(rights, axis=0).astype(jnp.float32)
    dest = routes[:, 0]
    pre = (
        jnp.dot(
            tokens,
            lax.all_gather(w_in, "dp", axis=0, tiled=True),
            preferred_element_type=jnp.float32,
        )
        + b_in
    )
    delta = hidden_grad.astype(jnp.float32) * slope(pre)
    left = jnp.dot(tokens, factors_in.T, preferred_element_type=jnp.float32)
    right = jnp.dot(delta, factors_hidden.T, precision=lax.Precision.HIGHEST)
    contrib = (left * right).reshape(tokens.shape[0], NB * QB, RANK).sum(axis=-1)
    keys = dest * EX_OUT + example_slot
    onehot_key = (keys[:, None] == jnp.arange(n_dp * EX_OUT, dtype=jnp.int32)[None, :]).astype(
        jnp.float32
    )
    terms = jnp.dot(onehot_key.T, contrib, precision=lax.Precision.HIGHEST)
    partial_value = lax.psum_scatter(terms, "dp", scatter_dimension=0, tiled=True)
    return lax.psum(partial_value, "mp")


def solution(mesh):
    in_specs = (
        P("dp", None),
        P("dp", "mp"),
        P("dp", "mp"),
        P("mp"),
        P("dp", None),
        P("dp", "mp"),
        P(),
        P("dp", None),
        P("dp"),
    )
    out_specs = P("dp", None)
    return jax.shard_map(body, mesh=mesh, in_specs=in_specs, out_specs=out_specs, check_vma=False)
```

profile of v0, /device:TPU:1, one launch (start us, length us, event | category | flops | bytes accessed | tf_op | source)
XLA Modules:
  0.0 804.2 jit_solution(16142879865291317622)
XLA Ops:
  6.5 0.0 copy-start
  6.5 0.0 all-gather.2.cloned.1.call-start
  6.6 0.7 all-gather.2.cloned.1.call-update
  7.3 0.0 all-reduce.4.cloned.1.call-start
  7.3 1.5 fusion.45
  11.4 1.6 broadcast_select_fusion.7
  12.9 2.0 broadcast_select_fusion.3
  14.9 0.0 all-reduce.4.cloned.1.call-update
  14.9 0.0 copy-done.2
  14.9 0.0 copy-done.1
  15.0 1.3 dynamic-slice
  16.9 0.0 copy-start.3
  16.9 127.2 %all-gather.2.cloned.1.call-done = bf16[4096,1024]{1,0:T(8,128)(2,1)} async-done(((bf16[64,1024]{1,0:T(8,128)(2,1)}), bf16[4096,1024]{1,0:T(8,128)(2,1)}) %all-gather.2.cloned.1.call-update) | async-done | bytes 8388624 | tf_op jit(solution)/shard_map/all_gather | solution.py:38
  144.1 0.0 copy-done
  144.1 0.0 copy-done.8
  144.1 6.8 convolution_add_fusion
  150.9 416.5 %all-reduce.4.cloned.1.call-done = (bf16[32,1024]{1,0:T(8,128)(2,1)}, bf16[32,1024]{1,0:T(8,128)(2,1)}, bf16[32,1024]{1,0:T(8,128)(2,1)}, bf16[32,1024]{1,0:T(8,...) async-done(((bf16[32,1024]{1,0:T(8,128)(2,1)}, bf16[32,1024]{1,0:T(8,128)(2,1)}, ...) | async-done | bytes 1310736 | tf_op jit(solution)/shard_map/psum | solution.py:14
  567.4 0.0 copy-done.3
  567.4 2.5 fusion.8
  569.9 0.0 copy-done.4
  570.0 0.9 fusion.2
  570.8 0.5 fusion.28
  571.4 205.3 %all-reduce = f32[512,16]{1,0:T(8,128)S(1)} all-reduce(f32[512,16]{1,0:T(8,128)S(1)} %fusion.28), channel_id=2, replica_groups=mesh['dp'=64,'mp'=8] {'dp'}, use_global_device_ids=true, to_apply=%region_9.10.clone | all-reduce | flops 8192 | bytes 65536
  776.7 20.6 %psum.71 = f32[8,16]{1,0:T(8,128)} all-reduce(f32[8,16]{1,0:T(8,128)S(1)} %constant_dynamic-slice_fusion), channel_id=1, replica_groups=mesh['dp'=64,'mp'=8] {'mp'}, use_global_device_ids=true, to_apply=%region_10.11 | all-reduce | flops 128 | bytes 1024 | tf_op jit(solution)/shard_map/psum | solution.py:53
  (13 shorter events, 0.0 us)
Async XLA Ops:
  6.5 137.6 %copy-start = (bf16[256,4096]{1,0:T(8,128)(2,1)S(1)}, bf16[256,4096]{1,0:T(8,128)(2,1)}, u32[]{:S(2)}) copy-start(bf16[256,4096]{1,0:T(8,128)(2,1)} %param.9) | copy-start | bytes 6291460
  6.5 8.4 %copy-start.2 = (s32[256,1]{0,1:T(1,128)S(1)}, s32[256,1]{0,1:T(1,128)}, u32[]{:S(2)}) copy-start(s32[256,1]{0,1:T(1,128)} %param.16) | copy-start | bytes 3076
  6.5 8.4 %copy-start.1 = (s32[256]{0:T(256)S(1)}, s32[256]{0:T(256)}, u32[]{:S(2)}) copy-start(s32[256]{0:T(256)} %param.17) | copy-start | bytes 3076
  6.5 137.6 %copy-start.8 = (f32[1024]{0:T(1024)S(1)}, f32[1024]{0:T(1024)}, u32[]{:S(2)}) copy-start(f32[1024]{0:T(1024)} %param.12) | copy-start | bytes 12292
  6.5 137.6 %all-gather.2.cloned.1.call-start = ((), (), s32[]{:S(2)}) async-start(), calls=%async_computation | async-start | bytes 8519680 | tf_op jit(solution)/shard_map/all_gather | solution.py:38
  7.3 560.1 %all-reduce.4.cloned.1.call-start = ((), (), s32[]{:S(2)}) async-start(), calls=%async_computation.1 | async-start | bytes 2621440 | tf_op jit(solution)/shard_map/psum | solution.py:14
  16.9 550.5 %copy-start.3 = (bf16[256,1024]{1,0:T(8,128)(2,1)S(1)}, bf16[256,1024]{1,0:T(8,128)(2,1)}, u32[]{:S(2)}) copy-start(bf16[256,1024]{1,0:T(8,128)(2,1)} %param.10) | copy-start | bytes 1572868
  567.4 2.5 copy-start.4
  567.4 2.5 copy-start.5
  567.4 2.5 copy-start.6
  567.4 2.5 copy-start.7
Sparse Core Ops, SparseCore 0:
  9.5 134.5 all-gather.1
  147.6 419.7 all-reduce.3
where the time goes:
time: 811 us; the launch traced here: 804 us
  waiting for transfers between devices  544 us (67%)
  blocking collectives  226 us (28%)
  between operations  16.8 us (2%)
  matrix products  10.6 us (1%)
    psum x1, waiting for transfers between devices, spread(): return lax.psum(kept, axis)  417 us
    unnamed x1, blocking collectives  205 us
    all_gather x1, waiting for transfers between devices, body(): lax.all_gather(w_in, 'dp', axis=0, tiled=True)  127 us
    psum x1, blocking collectives, body(): return lax.psum(partial_value, 'mp')  20.6 us
  transfers between devices with their start and end apart: 2, of which 2 were waited for; matrix products, arithmetic and copies ran while one was open for 2% of the time, Pallas kernels for 0%

commit v1 on v0

v1 whole, which is shorter than its diff:
```python
import functools

import jax
import jax.numpy as jnp
from jax import lax
from jax.experimental import pallas as pl
from jax.experimental.pallas import tpu as pltpu
from jax.sharding import PartitionSpec as P

MESH = pl.DeviceIdType.MESH
RANK = 8
EX_OUT = 8
NT = (((1,), (1,)), ((), ()))


def slope(pre):
    cdf = 0.5 * (1.0 + lax.erf(pre * 0.7071067811865476))
    dens = jnp.exp(-0.5 * pre * pre) * 0.3989422804014327
    return cdf + pre * dens


def kernel(
    X, YH, Z, NB,
    owners, tokens, hg, w, bias, qi, qh, meta, out,
    wbuf, tok2, acc, hg2, dhi, dlo, meta2,
    qi_raw, qh_raw, gbuf, rs_in, red, fbuf, fsib, fpair, left_all,
    terms, t1_in, psum, t2_in,
    ring_s, ring_r, sib_s, sib_r, tok_s, tok_r, pair_s, pair_r, quad_s, quad_r,
    rs_s, rs_r, ag_s, ag_r, fq_s, fq_r, lf_s, lf_r, t1_s, t1_r, t2_s, t2_r, loc_s,
):
    NY, S, NC = 2 * YH, Z // 2, 2 * NB
    T, D = tokens.shape
    WR, H = w.shape[0], w.shape[1] // 2
    QC = H // 2
    NPL = X * NY * 2
    R = Z // NC
    dp, mp = lax.axis_index("dp"), lax.axis_index("mp")
    c = lax.rem(dp, 2)
    z = lax.rem(lax.div(dp, 2), Z)
    yl = lax.div(dp, 2 * Z)
    yh = lax.rem(mp, YH)
    x = lax.div(mp, YH)
    y = yh * 2 + yl
    me_pl = (x * NY + y) * 2 + c
    quarter = yl * 2 + c

    def dev(x_, y_, z_, c_):
        return ((lax.rem(y_, 2) * Z + z_) * 2 + c_, x_ * YH + lax.div(y_, 2))

    def zpeer(k):
        return dev(x, y, lax.rem(z + k, Z), c)

    def plane(k):
        i = lax.rem(me_pl + k, NPL)
        return dev(lax.div(i, NY * 2), lax.rem(lax.div(i, 2), NY), z, lax.rem(i, 2))

    def remote(src, dst, send, recv, to):
        return pltpu.make_async_remote_copy(
            src_ref=src, dst_ref=dst, send_sem=send, recv_sem=recv,
            device_id=to, device_id_type=MESH,
        )

    def loop(n, f, start=0):
        def step(i, carry):
            f(i)
            return carry

        lax.fori_loop(start, n, step, 0)

    barrier = pltpu.get_barrier_semaphore()
    loop(Z, lambda k: pl.semaphore_signal(barrier, inc=1, device_id=zpeer(k), device_id_type=MESH), 1)
    loop(NPL, lambda k: pl.semaphore_signal(barrier, inc=1, device_id=plane(k), device_id_type=MESH), 1)
    pl.semaphore_wait(barrier, Z - 1 + NPL - 1)

    sibling = dev(x, y, z, 1 - c)
    partner = dev(x, yh * 2 + 1 - yl, z, c)
    up, down = zpeer(1), zpeer(Z - 1)
    y_up = dev(x, lax.rem(y + 1, NY), z, c)
    y_down = dev(x, lax.rem(y + NY - 1, NY), z, c)

    def half(i):
        return pl.ds(pl.multiple_of(i * H, H), H)

    pair_w = remote(w.at[:, half(1 - yl)], wbuf.at[z, yl, c], pair_s.at[0], pair_r.at[0], partner)
    pair_w.start()
    wbuf[z, yl, c] = w[:, half(yl)]

    def at(direction, s):
        return lax.rem(z + (Z - s if direction == 0 else s), Z)

    def ring(direction, a, s):
        ref = wbuf.at[at(direction, s - 1), a, c]
        return remote(
            ref, ref, ring_s.at[direction, a, s], ring_r.at[direction, a, s], (up, down)[direction]
        )

    def sib(direction, a, s):
        ref = wbuf.at[at(direction, s), a, c]
        return remote(ref, ref, sib_s.at[direction, a, s], sib_r.at[direction, a, s], sibling)

    def hops(direction, a):
        return S if direction == a else S - 1

    def cols(direction, s, h):
        return pl.ds(pl.multiple_of(h * (D // 2) + at(direction, s) * 2 * WR, 2 * WR), 2 * WR)

    def tok(direction, s, h):
        k = cols(direction, s, h)
        return remote(
            tokens.at[:, k], tok2.at[:, k], tok_s.at[direction, s, h], tok_r.at[direction, s, h],
            (y_up, y_down)[direction],
        )

    def tok_start(direction, s):
        if (1 if direction == 0 else 0) <= s <= (S if direction == 0 else S - 1):
            tok(direction, s, 0).start()
            tok(direction, s, 1).start()

    def first(a):
        ring(0, a, 1).start()
        ring(1, a, 1).start()
        sib(0, a, 0).start()

    first(yl)

    b_mine, h_mine = lax.div(mp, 2), lax.rem(mp, 2)
    qrows = pl.ds(pl.multiple_of(h_mine * 16, 16), 16)

    def quad_of(k):
        q = lax.rem(quarter + k, 4)
        return q, dev(x, yh * 2 + lax.div(q, 2), z, lax.rem(q, 2))

    def quad(k):
        q, to = quad_of(k)
        a = remote(
            qi.at[qrows, pl.ds(pl.multiple_of(q * (D // 4), 128), D // 4)], qi_raw.at[k],
            quad_s.at[0, k], quad_r.at[0, k], to,
        )
        b = remote(
            qh.at[:, pl.ds(pl.multiple_of(q * QC, 128), QC)], qh_raw.at[k],
            quad_s.at[1, k], quad_r.at[1, k], to,
        )
        return a, b

    for k in (1, 2, 3):
        for cp in quad(k):
            cp.start()
    qi_raw[0] = qi[qrows, pl.ds(pl.multiple_of(quarter * (D // 4), 128), D // 4)]
    qh_raw[0] = qh[:, pl.ds(pl.multiple_of(quarter * QC, 128), QC)]
    pair_meta = remote(meta, meta2, pair_s.at[1], pair_r.at[1], partner)
    pair_meta.start()

    pair_w.wait_recv()
    first(1 - yl)
    for s in (0, 1, 2):
        tok_start(0, s)
        tok_start(1, s)
    pair_hg = remote(hg.at[:, half(1 - yl)], hg2, pair_s.at[2], pair_r.at[2], partner)

    for k in (1, 2, 3):
        for cp in quad(k):
            cp.wait_recv()
    srcs = []
    for k in range(4):
        q = lax.rem(quarter + 4 - k, 4)
        srcs.append((lax.div(q, 2) * Z + z) * 2 + lax.rem(q, 2))

    def pick(b, k):
        return jnp.where(owners[b] == srcs[k], 1.0, 0.0).astype(jnp.float32)

    for i in range(NC):
        b, h = i // 2, i % 2
        gi = sum(pick(b_mine, k) * qi_raw[k, :, i * 128 : (i + 1) * 128].astype(jnp.float32) for k in range(4))
        gh = sum(pick(b, k) * qh_raw[k, h * 16 : (h + 1) * 16].astype(jnp.float32) for k in range(4))
        gbuf[i, :, :128] = gi.astype(jnp.bfloat16)
        gbuf[i, :, 128:] = gh.astype(jnp.bfloat16)

    is_red = lax.rem(z, R) == 0
    my_chunk = lax.div(z, R)

    def rs(i):
        k = lax.rem(z + Z - i * R, Z)
        return remote(gbuf.at[i], rs_in.at[k], rs_s.at[i], rs_r.at[k], dev(x, y, i * R, c))

    def rs_arrived(k):
        return remote(gbuf.at[0], rs_in.at[k], rs_s.at[0], rs_r.at[k], up)

    def ag(k):
        return remote(red, fbuf.at[my_chunk], ag_s.at[k], ag_r.at[my_chunk], zpeer(k))

    def ag_arrived(i):
        return remote(red, fbuf.at[i], ag_s.at[0], ag_r.at[i], up)

    def not_mine(f):
        def go(i):
            @pl.when(i * R != z)
            def _():
                f(i)

        return go

    loop(NC, not_mine(lambda i: rs(i).start()))

    def reduce_factors():
        @pl.when(is_red)
        def _():
            def add(k, total):
                rs_arrived(k).wait_recv()
                return total + rs_in[k].astype(jnp.float32)

            total = lax.fori_loop(1, Z, add, gbuf[my_chunk].astype(jnp.float32))
            red[...] = total.astype(jnp.bfloat16)
            fbuf[my_chunk] = total.astype(jnp.bfloat16)
            loop(Z, lambda k: ag(k).start(), 1)

    def fq(k):
        _, to = quad_of(k)
        return remote(fbuf.at[:, :, pl.ds(0, 128)], fpair.at[k - 1], fq_s.at[k], fq_r.at[k], to)

    fh_sib = remote(fbuf.at[:, :, pl.ds(128, QC)], fsib, fq_s.at[0], fq_r.at[0], sibling)

    def gather_factors():
        loop(NC, not_mine(lambda i: ag_arrived(i).wait_recv()))
        fh_sib.start()
        for k in (1, 2, 3):
            fq(k).start()

    def lf(k):
        n_y = NPL // 2
        i = lax.rem(lax.div(me_pl, 2) + k, n_y)
        to = dev(lax.div(i, NY), lax.rem(i, NY), z, c)
        ref = left_all.at[yl, mp]
        return remote(ref, ref, lf_s.at[k], lf_r.at[k], to)

    def lf_arrived(k):
        n_y = NPL // 2
        i = lax.rem(lax.div(me_pl, 2) + n_y - k, n_y)
        ref = left_all.at[lax.rem(i, 2), lax.div(i, NY) * YH + lax.div(lax.rem(i, NY), 2)]
        return remote(ref, ref, lf_s.at[k], lf_r.at[k], up)

    def left_part():
        total = jnp.zeros((16, T), jnp.float32)
        for k in range(4):
            q = lax.rem(quarter + 4 - k, 4)
            if k:
                fq(k).wait_recv()
            for i in range(NC):
                f = fbuf[i, :, :128] if k == 0 else fpair[k - 1, i]
                kk = pl.ds(pl.multiple_of(q * (D // 4) + i * 128, 128), 128)
                total = total + lax.dot_general(f, tokens[:, kk], NT, preferred_element_type=jnp.float32)
        left_all[yl, mp] = total
        loop(NPL // 2, lambda k: lf(k).start(), 1)

    def multiply(direction, s):
        for a in (0, 1):
            if s == 0:
                sib(0, a, 0).wait_recv()
            elif s <= hops(direction, a):
                sib(direction, a, s).wait_recv()
            elif s == S:
                sib(1 - direction, a, s).wait_recv()
        block = wbuf[at(direction, s)].reshape(4 * WR, H)
        k0, k1 = cols(direction, s, 0), cols(direction, s, 1)
        own = jnp.concatenate([tokens[:, k0], tokens[:, k1]], axis=1)
        acc[0] = acc[0] + jnp.dot(own, block, preferred_element_type=jnp.float32)
        tok(direction, s, 0).wait_recv()
        tok(direction, s, 1).wait_recv()
        other = jnp.concatenate([tok2[:, k0], tok2[:, k1]], axis=1)
        acc[1] = acc[1] + jnp.dot(other, block, preferred_element_type=jnp.float32)

    def advance(direction, a, s):
        if s <= hops(direction, a):
            ring(direction, a, s).wait_recv()
            if s + 1 <= hops(direction, a):
                ring(direction, a, s + 1).start()
            sib(direction, a, s).start()

    acc[...] = jnp.zeros_like(acc)
    for s in range(1, S + 1):
        for direction, a in ((0, 0), (1, 1), (0, 1), (1, 0)):
            advance(direction, a, s)
        if s + 2 <= S:
            tok_start(0, s + 2)
            tok_start(1, s + 2)
        if s == min(2, S):
            pair_hg.start()
        if s == min(3, S):
            reduce_factors()
        if s == min(5, S):
            gather_factors()
        if s == min(6, S):
            left_part()
        if s == 1:
            multiply(1, 0)
        else:
            multiply(0, s - 1)
            multiply(1, s - 1)
    multiply(0, S)

    pair_hg.wait_recv()
    pair_meta.wait_recv()
    fh_sib.wait_recv()
    fh_own = fbuf[:, :, 128:].reshape(NC * 16, QC)
    fh_other = fsib[...].reshape(NC * 16, QC)
    fh = jnp.concatenate([jnp.where(c == 0, fh_own, fh_other), jnp.where(c == 0, fh_other, fh_own)], axis=1)
    shift = bias[:, half(yl)]
    rows = 32
    for g in (0, 1):

        def some(i, carry, g=g):
            at_rows = pl.ds(pl.multiple_of(i * rows, rows), rows)
            grads = hg[at_rows, half(yl)] if g == 0 else hg2[at_rows, :]
            delta = grads.astype(jnp.float32) * slope(acc[g, at_rows, :] + shift)
            high = delta.astype(jnp.bfloat16)
            dhi[g, at_rows, :] = high
            dlo[g, at_rows, :] = (delta - high.astype(jnp.float32)).astype(jnp.bfloat16)
            return carry

        lax.fori_loop(0, T // rows, some, 0)
    loop(NPL // 2, lambda k: lf_arrived(k).wait_recv(), 1)
    total = jnp.zeros((Z * 4, 128), jnp.float32)
    n_q = NC * 16 // RANK
    for g in (0, 1):
        right = lax.dot_general(fh, dhi[g], NT, preferred_element_type=jnp.float32)
        right = right + lax.dot_general(fh, dlo[g], NT, preferred_element_type=jnp.float32)
        left = left_all[yl if g == 0 else 1 - yl].reshape(NC * 16, T)
        contrib = (left * right).reshape(n_q, RANK, T).sum(axis=1)
        keys = meta[...] if g == 0 else meta2[...]
        wide = jnp.concatenate([contrib] * (128 // n_q), axis=0)
        slot_of = lax.div(lax.broadcasted_iota(jnp.int32, (128, T), 0), n_q)
        wide = jnp.where(slot_of == keys[1:2], wide, 0.0)
        place = lax.broadcasted_iota(jnp.int32, (Z * 4, T), 0)
        named = jnp.where(place == keys[0:1], 1.0, 0.0).astype(jnp.bfloat16)
        high = wide.astype(jnp.bfloat16)
        rest = wide - high.astype(jnp.float32)
        mid = rest.astype(jnp.bfloat16)
        low = (rest - mid.astype(jnp.float32)).astype(jnp.bfloat16)
        for part in (high, mid, low):
            total = total + lax.dot_general(named, part, NT, preferred_element_type=jnp.float32)
    for i in range(Z):
        terms[i] = total[i * 4 : i * 4 + 4]

    def t1(k):
        return remote(terms.at[lax.rem(z + k, Z)], t1_in.at[k], t1_s.at[k], t1_r.at[k], zpeer(k))

    def t2(k):
        return remote(psum, t2_in.at[k], t2_s.at[k], t2_r.at[k], plane(k))

    loop(Z, lambda k: t1(k).start(), 1)

    def add1(k, total):
        t1(k).wait_recv()
        return total + t1_in[k]

    mine = lax.fori_loop(1, Z, add1, terms[z])
    psum[...] = mine
    loop(NPL, lambda k: t2(k).start(), 1)

    def add2(k, total):
        t2(k).wait_recv()
        return total + t2_in[k]

    mine = lax.fori_loop(1, NPL, add2, mine)
    row = lax.broadcasted_iota(jnp.int32, (4, 128), 0)
    out[...] = jnp.sum(jnp.where(row == quarter, mine, 0.0), axis=0, keepdims=True)

    for cp in (pair_w, pair_meta, pair_hg, fh_sib):
        cp.wait_send()
    for direction in (0, 1):
        for a in (0, 1):
            for s in range(1, hops(direction, a) + 1):
                ring(direction, a, s).wait_send()
                sib(direction, a, s).wait_send()
    for a in (0, 1):
        sib(0, a, 0).wait_send()
    for direction in (0, 1):
        for s in range(1 - direction, S + 1 - direction):
            for h in (0, 1):
                tok(direction, s, h).wait_send()
    for k in (1, 2, 3):
        for cp in quad(k):
            cp.wait_send()
        fq(k).wait_send()
    loop(NC, not_mine(lambda i: rs(i).wait_send()))

    @pl.when(is_red)
    def _():
        loop(Z, lambda k: ag(k).wait_send(), 1)

    loop(NPL // 2, lambda k: lf(k).wait_send(), 1)
    loop(Z, lambda k: t1(k).wait_send(), 1)
    loop(NPL, lambda k: t2(k).wait_send(), 1)


def body(X, YH, Z, tokens, hidden_grad, w_in, b_in, query_in, query_hidden, owners, routes, example_slot):
    T, D = tokens.shape
    M = query_in.shape[0]
    NB = X * YH * 16 // M
    H = w_in.shape[1] // 2
    QC = H // 2
    NC = 2 * NB
    NY, S = 2 * YH, Z // 2
    NPL = X * NY * 2
    dest = routes[:, 0]
    place = lax.rem(lax.div(dest, 2), Z) * 4 + lax.div(dest, 2 * Z) * 2 + lax.rem(dest, 2)
    meta = jnp.concatenate([place[None], example_slot[None], jnp.zeros((6, T), jnp.int32)])
    bf, f32 = jnp.bfloat16, jnp.float32
    dma = pltpu.SemaphoreType.DMA
    vmem = pl.BlockSpec(memory_space=pltpu.VMEM)
    scratch = [
        pltpu.VMEM((Z, 2, 2, w_in.shape[0], H), bf),
        pltpu.VMEM((T, D), bf),
        pltpu.VMEM((2, T, H), f32),
        pltpu.VMEM((T, H), bf),
        pltpu.VMEM((2, T, H), bf),
        pltpu.VMEM((2, T, H), bf),
        pltpu.VMEM((8, T), jnp.int32),
        pltpu.VMEM((4, 16, D // 4), bf),
        pltpu.VMEM((4, M, QC), bf),
        pltpu.VMEM((NC, 16, 128 + QC), bf),
        pltpu.VMEM((Z, 16, 128 + QC), bf),
        pltpu.VMEM((16, 128 + QC), bf),
        pltpu.VMEM((NC, 16, 128 + QC), bf),
        pltpu.VMEM((NC, 16, QC), bf),
        pltpu.VMEM((3, NC, 16, 128), bf),
        pltpu.VMEM((2, X * YH, 16, T), f32),
        pltpu.VMEM((Z, 4, 128), f32),
        pltpu.VMEM((Z, 4, 128), f32),
        pltpu.VMEM((4, 128), f32),
        pltpu.VMEM((NPL, 4, 128), f32),
    ]
    scratch += [dma((2, 2, S + 1))] * 4 + [dma((2, S + 1, 2))] * 2 + [dma((3,))] * 2
    scratch += [dma((2, 4))] * 2 + [dma((NC,)), dma((Z,)), dma((Z,)), dma((NC,))] + [dma((4,))] * 2
    scratch += [dma((NPL // 2,))] * 2 + [dma((Z,))] * 2 + [dma((NPL,))] * 2 + [dma((1,))]
    scores = pl.pallas_call(
        functools.partial(kernel, X, YH, Z, NB),
        out_shape=jax.ShapeDtypeStruct((1, 128), f32),
        in_specs=[pl.BlockSpec(memory_space=pltpu.SMEM)] + [vmem] * 7,
        out_specs=vmem,
        scratch_shapes=scratch,
        compiler_params=pltpu.CompilerParams(
            collective_id=0, has_side_effects=True, vmem_limit_bytes=48 * 2**20
        ),
    )(owners, tokens, hidden_grad, w_in, b_in[None], query_in, query_hidden, meta)
    n_q = NC * 16 // RANK
    return scores[:, : EX_OUT * n_q].reshape(EX_OUT, n_q)


def solution(mesh, YH=2):
    Z = mesh.shape["dp"] // 4
    X = mesh.shape["mp"] // YH
    in_specs = (
        P("dp", None), P("dp", "mp"), P("dp", "mp"), P("mp"), P("dp", None), P("dp", "mp"), P(),
        P("dp", None), P("dp"),
    )
    return jax.shard_map(
        functools.partial(body, X, YH, Z), mesh=mesh, in_specs=in_specs, out_specs=P("dp", None), check_vma=False
    )
```

time: 811 us -> 90.7 us (0.11)
  waiting for transfers between devices: 544 us -> 0 us
  blocking collectives: 226 us -> 0 us
  Pallas kernels: 0 us -> 80.3 us
  between operations: 16.8 us -> 0.03 us
  matrix products: 10.6 us -> 0 us
    psum x1 -> x0, waiting for transfers between devices: 417 us -> none  [spread(): return lax.psum(kept, axis)]
    unnamed x1 -> x0, blocking collectives: 205 us -> none
    all_gather x1 -> x0, waiting for transfers between devices: 127 us -> none  [body(): lax.all_gather(w_in, 'dp', axis=0, tiled=True)]
    pallas_call x0 -> x1, Pallas kernels: none -> 80.3 us  [body(): pl.pallas_call(functools.partial(kernel, X, YH, Z, NB), out_shape=jax.Sha...]
    psum x1 -> x0, blocking collectives: 20.6 us -> none  [body(): return lax.psum(partial_value, 'mp')]
    dot_general x4 -> x0, matrix products: 10.6 us -> none  [the longest x1 6.77 us: body(): jnp.dot(tokens, lax.all_gather(w_in, 'dp', axis=0, tiled=True), preferred...]
  transfers between devices with their start and end apart: 2 -> 0, of which waited for: 2 -> 0; matrix products, arithmetic and copies ran while one was open for 2% -> 0% of each run, Pallas kernels for 0% -> 0%
where the time goes in v1:
time: 90.7 us; the launch traced here: 90.3 us
  Pallas kernels  80.3 us (89%)
  local copies, waits for them, and re-layouts  7.93 us (9%)
  other arithmetic  2.1 us (2%)
    pallas_call x1, Pallas kernels, body(): pl.pallas_call(functools.partial(kernel, X, YH, Z, NB), out_shape=jax.Sha...  80.3 us
    unnamed x14, local copies, waits for them, and re-layouts  6.66 us

profile of v1, /device:TPU:1, one launch (start us, length us, event | category | flops | bytes accessed | tf_op | source)
XLA Modules:
  0.0 90.3 jit_solution(6069081968999795124)
XLA Ops:
  0.0 0.7 fusion.2
  0.7 0.1 pad.2.clone
  0.8 0.7 add_add_fusion.meta
  1.5 0.0 copy-start
  1.5 1.6 %copy-done = bf16[256,4096]{1,0:T(8,128)(2,1)S(1)} copy-done((bf16[256,4096]{1,0:T(8,128)(2,1)S(1)}, bf16[256,4096]{1,0:T(8,128)(2,1)}, u32[]{:S(2)}) %copy-start) | copy-done | bytes 2097176
  3.1 0.0 copy-start.1
  3.1 1.0 %copy-done.1 = bf16[256,1024]{1,0:T(8,128)(2,1)S(1)} copy-done((bf16[256,1024]{1,0:T(8,128)(2,1)S(1)}, bf16[256,1024]{1,0:T(8,128)(2,1)}, u32[]{:S(2)}) %copy-start.1) | copy-done | bytes 524312
  4.2 0.0 copy-start.2
  4.2 0.9 %copy-done.2 = bf16[32,4096]{1,0:T(8,128)(2,1)S(1)} copy-done((bf16[32,4096]{1,0:T(8,128)(2,1)S(1)}, bf16[32,4096]{1,0:T(8,128)(2,1)}, u32[]{:S(2)}) %copy-start.2) | copy-done | bytes 262168
  5.1 0.0 copy-start.3
  5.1 0.9 copy-done.3
  6.0 0.0 copy-start.4
  6.0 0.8 copy-done.4
  6.9 0.0 copy-start.5
  6.9 0.7 copy-done.5
  7.5 0.0 copy-start.6
  7.5 0.7 copy-done.6
  8.2 80.3 %shard_map.91 = f32[1,128]{1,0:T(1,128)S(1)} custom-call(s32[64]{0:T(128)S(1)} %copy-done.6, bf16[256,4096]{1,0:T(8,128)(2,1)S(1)} %copy-done, bf16[256,1024]{1,0:T(8,128)(2,1)S(1)} %copy-done.1, bf16[64,1024]{1,0:T(8,128)(2,1)S(1)} %copy-done.3, f32[1,1024]{1,0:T(1,128)S(1)} %bitcast.15, bf16[32,4096]{1,0:T(8,128)(2,1)S(1)} %copy-done.2, ...), custom_call_target="tpu_custom_call" | custom-call | tf_op jit(solution)/shard_map/pallas_call | solution.py:435
  88.5 0.5 broadcast.76
  89.0 0.7 reduce.3
  89.6 0.7 reshape.88
  (1 shorter events, 0.0 us)
Async XLA Ops:
  1.5 1.6 %copy-start = (bf16[256,4096]{1,0:T(8,128)(2,1)S(1)}, bf16[256,4096]{1,0:T(8,128)(2,1)}, u32[]{:S(2)}) copy-start(bf16[256,4096]{1,0:T(8,128)(2,1)} %tokens.1) | copy-start | bytes 6291460
  3.1 1.0 %copy-start.1 = (bf16[256,1024]{1,0:T(8,128)(2,1)S(1)}, bf16[256,1024]{1,0:T(8,128)(2,1)}, u32[]{:S(2)}) copy-start(bf16[256,1024]{1,0:T(8,128)(2,1)} %hg.1) | copy-start | bytes 1572868
  4.2 0.9 %copy-start.2 = (bf16[32,4096]{1,0:T(8,128)(2,1)S(1)}, bf16[32,4096]{1,0:T(8,128)(2,1)}, u32[]{:S(2)}) copy-start(bf16[32,4096]{1,0:T(8,128)(2,1)} %qi.1) | copy-start | bytes 786436
  5.1 0.9 %copy-start.3 = (bf16[64,1024]{1,0:T(8,128)(2,1)S(1)}, bf16[64,1024]{1,0:T(8,128)(2,1)}, u32[]{:S(2)}) copy-start(bf16[64,1024]{1,0:T(8,128)(2,1)} %w.1) | copy-start | bytes 393220
  6.0 0.8 copy-start.4
  6.9 0.7 copy-start.5
  7.5 0.7 copy-start.6

commit v2 on v1

--- a/solution.py
+++ b/solution.py
@@ -21,15 +21,16 @@
 
 def kernel(
     X, YH, Z, NB,
-    owners, tokens, hg, w, bias, qi, qh, meta, out,
-    wbuf, tok2, acc, hg2, dhi, dlo, meta2,
+    owners_in, tok_in, hg_in, w, bias_in, qi, qh, routes, slots, out,
+    owners, tokens, hg, bias, keys,
+    wbuf, tok2, acc, hg2, dhi, dlo,
     qi_raw, qh_raw, gbuf, rs_in, red, fbuf, fsib, fpair, left_all,
     terms, t1_in, psum, t2_in,
     ring_s, ring_r, sib_s, sib_r, tok_s, tok_r, pair_s, pair_r, quad_s, quad_r,
-    rs_s, rs_r, ag_s, ag_r, fq_s, fq_r, lf_s, lf_r, t1_s, t1_r, t2_s, t2_r, loc_s,
+    rs_s, rs_r, ag_s, ag_r, fq_s, fq_r, lf_s, lf_r, t1_s, t1_r, t2_s, t2_r, loc_s, know,
 ):
     NY, S, NC = 2 * YH, Z // 2, 2 * NB
-    T, D = tokens.shape
+    T, D = tok_in.shape
     WR, H = w.shape[0], w.shape[1] // 2
     QC = H // 2
     NPL = X * NY * 2
@@ -67,10 +68,46 @@
 
         lax.fori_loop(start, n, step, 0)
 
+    b_mine, h_mine = lax.div(mp, 2), lax.rem(mp, 2)
+    qrows = pl.ds(pl.multiple_of(h_mine * 16, 16), 16)
+
+    def half(i):
+        return pl.ds(pl.multiple_of(i * H, H), H)
+
+    locals_ = [
+        (w.at[:, half(yl)], wbuf.at[z, yl, c]),
+        (qi.at[qrows, pl.ds(pl.multiple_of(quarter * (D // 4), 128), D // 4)], qi_raw.at[0]),
+        (qh.at[:, pl.ds(pl.multiple_of(quarter * QC, 128), QC)], qh_raw.at[0]),
+        (owners_in, owners),
+        (tok_in, tokens),
+        (hg_in.at[:, half(yl)], hg),
+        (bias_in.at[:, half(yl)], bias),
+        (routes, keys.at[0]),
+        (slots, keys.at[1]),
+    ]
+    own = [pltpu.make_async_copy(src, dst, loc_s.at[i]) for i, (src, dst) in enumerate(locals_)]
+    for cp in own:
+        cp.start()
+
+    def steps(n, k):
+        return sorted({k % n, -k % n} - {0}) if k < n else []
+
+    def circle(kx, ky, kz, core):
+        found = [dev(lax.rem(x + k, X), y, z, c) for k in (steps(X, kx) if kx else [])]
+        found += [dev(x, lax.rem(y + k, NY), z, c) for k in (steps(NY, ky) if ky else [])]
+        found += [zpeer(k) for k in (steps(Z, kz) if kz else [])]
+        return found + ([dev(x, y, z, 1 - c)] if core else [])
+
+    def tell(sem, devices):
+        for to in devices:
+            pl.semaphore_signal(sem, inc=1, device_id=to, device_id_type=MESH)
+
+    near = circle(1, 1, 1, True)
+    far2 = circle(2, 2, 2, True)
+    far4 = circle(0, 0, 4, True)
     barrier = pltpu.get_barrier_semaphore()
-    loop(Z, lambda k: pl.semaphore_signal(barrier, inc=1, device_id=zpeer(k), device_id_type=MESH), 1)
-    loop(NPL, lambda k: pl.semaphore_signal(barrier, inc=1, device_id=plane(k), device_id_type=MESH), 1)
-    pl.semaphore_wait(barrier, Z - 1 + NPL - 1)
+    tell(barrier, near)
+    pl.semaphore_wait(barrier, len(near))
 
     sibling = dev(x, y, z, 1 - c)
     partner = dev(x, yh * 2 + 1 - yl, z, c)
@@ -78,12 +115,9 @@
     y_up = dev(x, lax.rem(y + 1, NY), z, c)
     y_down = dev(x, lax.rem(y + NY - 1, NY), z, c)
 
-    def half(i):
-        return pl.ds(pl.multiple_of(i * H, H), H)
-
     pair_w = remote(w.at[:, half(1 - yl)], wbuf.at[z, yl, c], pair_s.at[0], pair_r.at[0], partner)
     pair_w.start()
-    wbuf[z, yl, c] = w[:, half(yl)]
+    own[0].wait()
 
     def at(direction, s):
         return lax.rem(z + (Z - s if direction == 0 else s), Z)
@@ -122,9 +156,7 @@
         sib(0, a, 0).start()
 
     first(yl)
-
-    b_mine, h_mine = lax.div(mp, 2), lax.rem(mp, 2)
-    qrows = pl.ds(pl.multiple_of(h_mine * 16, 16), 16)
+    tell(know.at[0], near)
 
     def quad_of(k):
         q = lax.rem(quarter + k, 4)
@@ -142,38 +174,45 @@
         )
         return a, b
 
+    pair_routes = remote(routes, keys.at[2], pair_s.at[1], pair_r.at[1], partner)
+    pair_routes.start()
+    pair_slots = remote(slots, keys.at[3], pair_s.at[3], pair_r.at[3], partner)
+    pair_slots.start()
+
+    pair_w.wait_recv()
+    first(1 - yl)
+    own[4].wait()
+    for s in (0, 1, 2):
+        tok_start(0, s)
+        tok_start(1, s)
+    pair_hg = remote(hg_in.at[:, half(1 - yl)], hg2, pair_s.at[2], pair_r.at[2], partner)
+
+    pl.semaphore_wait(know.at[0], len(near))
     for k in (1, 2, 3):
         for cp in quad(k):
             cp.start()
-    qi_raw[0] = qi[qrows, pl.ds(pl.multiple_of(quarter * (D // 4), 128), D // 4)]
-    qh_raw[0] = qh[:, pl.ds(pl.multiple_of(quarter * QC, 128), QC)]
-    pair_meta = remote(meta, meta2, pair_s.at[1], pair_r.at[1], partner)
-    pair_meta.start()
-
-    pair_w.wait_recv()
-    first(1 - yl)
-    for s in (0, 1, 2):
-        tok_start(0, s)
-        tok_start(1, s)
-    pair_hg = remote(hg.at[:, half(1 - yl)], hg2, pair_s.at[2], pair_r.at[2], partner)
-
-    for k in (1, 2, 3):
-        for cp in quad(k):
-            cp.wait_recv()
-    srcs = []
-    for k in range(4):
-        q = lax.rem(quarter + 4 - k, 4)
-        srcs.append((lax.div(q, 2) * Z + z) * 2 + lax.rem(q, 2))
-
-    def pick(b, k):
-        return jnp.where(owners[b] == srcs[k], 1.0, 0.0).astype(jnp.float32)
-
-    for i in range(NC):
-        b, h = i // 2, i % 2
-        gi = sum(pick(b_mine, k) * qi_raw[k, :, i * 128 : (i + 1) * 128].astype(jnp.float32) for k in range(4))
-        gh = sum(pick(b, k) * qh_raw[k, h * 16 : (h + 1) * 16].astype(jnp.float32) for k in range(4))
-        gbuf[i, :, :128] = gi.astype(jnp.bfloat16)
-        gbuf[i, :, 128:] = gh.astype(jnp.bfloat16)
+    tell(know.at[1], far2)
+
+    def pick_factors():
+        for k in (1, 2, 3):
+            for cp in quad(k):
+                cp.wait_recv()
+        for i in (1, 2, 3):
+            own[i].wait()
+        srcs = []
+        for k in range(4):
+            q = lax.rem(quarter + 4 - k, 4)
+            srcs.append((lax.div(q, 2) * Z + z) * 2 + lax.rem(q, 2))
+
+        def pick(b, k):
+            return jnp.where(owners[b] == srcs[k], 1.0, 0.0).astype(jnp.float32)
+
+        for i in range(NC):
+            b, h = i // 2, i % 2
+            gi = sum(pick(b_mine, k) * qi_raw[k, :, i * 128 : (i + 1) * 128].astype(jnp.float32) for k in range(4))
+            gh = sum(pick(b, k) * qh_raw[k, h * 16 : (h + 1) * 16].astype(jnp.float32) for k in range(4))
+            gbuf[i, :, :128] = gi.astype(jnp.bfloat16)
+            gbuf[i, :, 128:] = gh.astype(jnp.bfloat16)
 
     is_red = lax.rem(z, R) == 0
     my_chunk = lax.div(z, R)
@@ -198,8 +237,6 @@
                 f(i)
 
         return go
-
-    loop(NC, not_mine(lambda i: rs(i).start()))
 
     def reduce_factors():
         @pl.when(is_red)
@@ -282,34 +319,46 @@
         if s + 2 <= S:
             tok_start(0, s + 2)
             tok_start(1, s + 2)
+        if s == 1:
+            pl.semaphore_wait(know.at[1], len(far2))
+            tell(know.at[2], far4)
+            pick_factors()
         if s == min(2, S):
+            pl.semaphore_wait(know.at[2], len(far4))
+            loop(NC, not_mine(lambda i: rs(i).start()))
             pair_hg.start()
-        if s == min(3, S):
+        if s == min(5, S):
             reduce_factors()
-        if s == min(5, S):
-            gather_factors()
-        if s == min(6, S):
-            left_part()
-        if s == 1:
+        if s == 2:
             multiply(1, 0)
-        else:
-            multiply(0, s - 1)
-            multiply(1, s - 1)
+        elif s > 2:
+            multiply(0, s - 2)
+            multiply(1, s - 2)
+    if S == 1:
+        multiply(1, 0)
+    else:
+        multiply(0, S - 1)
+        multiply(1, S - 1)
+    gather_factors()
+    left_part()
     multiply(0, S)
 
     pair_hg.wait_recv()
-    pair_meta.wait_recv()
+    pair_routes.wait_recv()
+    pair_slots.wait_recv()
+    for i in (5, 6, 7, 8):
+        own[i].wait()
     fh_sib.wait_recv()
     fh_own = fbuf[:, :, 128:].reshape(NC * 16, QC)
     fh_other = fsib[...].reshape(NC * 16, QC)
     fh = jnp.concatenate([jnp.where(c == 0, fh_own, fh_other), jnp.where(c == 0, fh_other, fh_own)], axis=1)
-    shift = bias[:, half(yl)]
+    shift = bias[...]
     rows = 32
     for g in (0, 1):
 
         def some(i, carry, g=g):
             at_rows = pl.ds(pl.multiple_of(i * rows, rows), rows)
-            grads = hg[at_rows, half(yl)] if g == 0 else hg2[at_rows, :]
+            grads = hg[at_rows, :] if g == 0 else hg2[at_rows, :]
             delta = grads.astype(jnp.float32) * slope(acc[g, at_rows, :] + shift)
             high = delta.astype(jnp.bfloat16)
             dhi[g, at_rows, :] = high
@@ -319,18 +368,20 @@
         lax.fori_loop(0, T // rows, some, 0)
     loop(NPL // 2, lambda k: lf_arrived(k).wait_recv(), 1)
     total = jnp.zeros((Z * 4, 128), jnp.float32)
+    bits = Z.bit_length()
     n_q = NC * 16 // RANK
     for g in (0, 1):
         right = lax.dot_general(fh, dhi[g], NT, preferred_element_type=jnp.float32)
         right = right + lax.dot_general(fh, dlo[g], NT, preferred_element_type=jnp.float32)
         left = left_all[yl if g == 0 else 1 - yl].reshape(NC * 16, T)
         contrib = (left * right).reshape(n_q, RANK, T).sum(axis=1)
-        keys = meta[...] if g == 0 else meta2[...]
+        dest, slot = keys[2 * g], keys[2 * g + 1]
+        there = (dest >> 1 & Z - 1) * 4 + (dest >> bits) * 2 + (dest & 1)
         wide = jnp.concatenate([contrib] * (128 // n_q), axis=0)
         slot_of = lax.div(lax.broadcasted_iota(jnp.int32, (128, T), 0), n_q)
-        wide = jnp.where(slot_of == keys[1:2], wide, 0.0)
+        wide = jnp.where(slot_of == slot, wide, 0.0)
         place = lax.broadcasted_iota(jnp.int32, (Z * 4, T), 0)
-        named = jnp.where(place == keys[0:1], 1.0, 0.0).astype(jnp.bfloat16)
+        named = jnp.where(place == there, 1.0, 0.0).astype(jnp.bfloat16)
         high = wide.astype(jnp.bfloat16)
         rest = wide - high.astype(jnp.float32)
         mid = rest.astype(jnp.bfloat16)
@@ -362,9 +413,11 @@
 
     mine = lax.fori_loop(1, NPL, add2, mine)
     row = lax.broadcasted_iota(jnp.int32, (4, 128), 0)
-    out[...] = jnp.sum(jnp.where(row == quarter, mine, 0.0), axis=0, keepdims=True)
-
-    for cp in (pair_w, pair_meta, pair_hg, fh_sib):
+    scores = jnp.sum(jnp.where(row == quarter, mine, 0.0), axis=0, keepdims=True)
+    for e in range(EX_OUT):
+        out[e : e + 1, :] = scores[:, e * n_q : (e + 1) * n_q]
+
+    for cp in (pair_w, pair_routes, pair_slots, pair_hg, fh_sib):
         cp.wait_send()
     for direction in (0, 1):
         for a in (0, 1):
@@ -401,20 +454,22 @@
     NC = 2 * NB
     NY, S = 2 * YH, Z // 2
     NPL = X * NY * 2
-    dest = routes[:, 0]
-    place = lax.rem(lax.div(dest, 2), Z) * 4 + lax.div(dest, 2 * Z) * 2 + lax.rem(dest, 2)
-    meta = jnp.concatenate([place[None], example_slot[None], jnp.zeros((6, T), jnp.int32)])
     bf, f32 = jnp.bfloat16, jnp.float32
     dma = pltpu.SemaphoreType.DMA
     vmem = pl.BlockSpec(memory_space=pltpu.VMEM)
+    anywhere = pl.BlockSpec(memory_space=pl.ANY)
     scratch = [
+        pltpu.SMEM(owners.shape, jnp.int32),
+        pltpu.VMEM((T, D), bf),
+        pltpu.VMEM((T, H), bf),
+        pltpu.VMEM((1, H), f32),
+        pltpu.VMEM((4, 1, T), jnp.int32),
         pltpu.VMEM((Z, 2, 2, w_in.shape[0], H), bf),
         pltpu.VMEM((T, D), bf),
         pltpu.VMEM((2, T, H), f32),
         pltpu.VMEM((T, H), bf),
         pltpu.VMEM((2, T, H), bf),
         pltpu.VMEM((2, T, H), bf),
-        pltpu.VMEM((8, T), jnp.int32),
         pltpu.VMEM((4, 16, D // 4), bf),
         pltpu.VMEM((4, M, QC), bf),
         pltpu.VMEM((NC, 16, 128 + QC), bf),
@@ -429,21 +484,19 @@
         pltpu.VMEM((4, 128), f32),
         pltpu.VMEM((NPL, 4, 128), f32),
     ]
-    scratch += [dma((2, 2, S + 1))] * 4 + [dma((2, S + 1, 2))] * 2 + [dma((3,))] * 2
+    scratch += [dma((2, 2, S + 1))] * 4 + [dma((2, S + 1, 2))] * 2 + [dma((4,))] * 2
     scratch += [dma((2, 4))] * 2 + [dma((NC,)), dma((Z,)), dma((Z,)), dma((NC,))] + [dma((4,))] * 2
-    scratch += [dma((NPL // 2,))] * 2 + [dma((Z,))] * 2 + [dma((NPL,))] * 2 + [dma((1,))]
-    scores = pl.pallas_call(
+    scratch += [dma((NPL // 2,))] * 2 + [dma((Z,))] * 2 + [dma((NPL,))] * 2 + [dma((9,)), pltpu.SemaphoreType.REGULAR((3,))]
+    return pl.pallas_call(
         functools.partial(kernel, X, YH, Z, NB),
-        out_shape=jax.ShapeDtypeStruct((1, 128), f32),
-        in_specs=[pl.BlockSpec(memory_space=pltpu.SMEM)] + [vmem] * 7,
+        out_shape=jax.ShapeDtypeStruct((EX_OUT, NC * 16 // RANK), f32),
+        in_specs=[anywhere] * 9,
         out_specs=vmem,
         scratch_shapes=scratch,
         compiler_params=pltpu.CompilerParams(
-            collective_id=0, has_side_effects=True, vmem_limit_bytes=48 * 2**20
+            collective_id=0, has_side_effects=True, vmem_limit_bytes=60 * 2**20
         ),
-    )(owners, tokens, hidden_grad, w_in, b_in[None], query_in, query_hidden, meta)
-    n_q = NC * 16 // RANK
-    return scores[:, : EX_OUT * n_q].reshape(EX_OUT, n_q)
+    )(owners, tokens, hidden_grad, w_in, b_in[None], query_in, query_hidden, routes.reshape(1, T), example_slot[None])
 
 
 def solution(mesh, YH=2):

time: 90.7 us -> 91.4 us (level)
  Pallas kernels: 80.3 us -> 90 us
  local copies, waits for them, and re-layouts: 7.93 us -> 1.28 us
  other arithmetic: 2.1 us -> 0 us
    pallas_call x1, Pallas kernels: 80.3 us -> 90 us  [body(): pl.pallas_call(functools.partial(kernel, X, YH, Z, NB), out_shape=jax.Sha...]
    unnamed x14 -> x1, local copies, waits for them, and re-layouts: 6.66 us -> 1.28 us
where the time goes in v2:
time: 91.4 us; the launch traced here: 91.3 us
  Pallas kernels  90 us (98%)
  local copies, waits for them, and re-layouts  1.28 us (1%)
    pallas_call x1, Pallas kernels, body(): pl.pallas_call(functools.partial(kernel, X, YH, Z, NB), out_shape=jax.Sha...  90 us

profile of v2, /device:TPU:1, one launch (start us, length us, event | category | flops | bytes accessed | tf_op | source)
XLA Modules:
  0.0 91.3 jit_solution(16334402628998628043)
XLA Ops:
  0.0 90.0 %shard_map.91 = f32[8,16]{1,0:T(8,128)} custom-call(s32[64]{0:T(128)} %owners_in.1, bf16[256,4096]{1,0:T(8,128)(2,1)} %tok_in.1, bf16[256,1024]{1,0:T(8,128)(2,1)} %hg_in.1, bf16[64,1024]{1,0:T(8,128)(2,1)} %w.1, f32[1,1024]{1,0:T(1,128)} %bitcast.3, bf16[32,4096]{1,0:T(8,128)(2,1)} %qi.1, bf16[32,1024]{1,0:T(8,128)(2,1)} %qh.1, s32[1,256]{1,0:T(1,128)} %bitcast.4, ...), custom_call_target="tpu_custom_call" | custom-call | tf_op jit(solution)/shard_map/pallas_call | solution.py:490
  90.0 1.3 %copy.11 = f32[8,16]{1,0:T(8,128)} copy(f32[8,16]{1,0:T(8,128)} %shard_map.91) | data formatting | bytes 1024

commit v3 on v1

--- a/solution.py
+++ b/solution.py
@@ -21,15 +21,16 @@
 
 def kernel(
     X, YH, Z, NB,
-    owners, tokens, hg, w, bias, qi, qh, meta, out,
-    wbuf, tok2, acc, hg2, dhi, dlo, meta2,
+    owners_in, tok_in, hg_in, w, bias_in, qi, qh, routes, slots, out,
+    owners, tokens, hg, bias, keys,
+    wbuf, tok2, acc, hg2, dhi, dlo,
     qi_raw, qh_raw, gbuf, rs_in, red, fbuf, fsib, fpair, left_all,
     terms, t1_in, psum, t2_in,
     ring_s, ring_r, sib_s, sib_r, tok_s, tok_r, pair_s, pair_r, quad_s, quad_r,
     rs_s, rs_r, ag_s, ag_r, fq_s, fq_r, lf_s, lf_r, t1_s, t1_r, t2_s, t2_r, loc_s,
 ):
     NY, S, NC = 2 * YH, Z // 2, 2 * NB
-    T, D = tokens.shape
+    T, D = tok_in.shape
     WR, H = w.shape[0], w.shape[1] // 2
     QC = H // 2
     NPL = X * NY * 2
@@ -67,6 +68,27 @@
 
         lax.fori_loop(start, n, step, 0)
 
+    b_mine, h_mine = lax.div(mp, 2), lax.rem(mp, 2)
+    qrows = pl.ds(pl.multiple_of(h_mine * 16, 16), 16)
+
+    def half(i):
+        return pl.ds(pl.multiple_of(i * H, H), H)
+
+    locals_ = [
+        (w.at[:, half(yl)], wbuf.at[z, yl, c]),
+        (qi.at[qrows, pl.ds(pl.multiple_of(quarter * (D // 4), 128), D // 4)], qi_raw.at[0]),
+        (qh.at[:, pl.ds(pl.multiple_of(quarter * QC, 128), QC)], qh_raw.at[0]),
+        (owners_in, owners),
+        (tok_in, tokens),
+        (hg_in.at[:, half(yl)], hg),
+        (bias_in.at[:, half(yl)], bias),
+        (routes, keys.at[0]),
+        (slots, keys.at[1]),
+    ]
+    own = [pltpu.make_async_copy(src, dst, loc_s.at[i]) for i, (src, dst) in enumerate(locals_)]
+    for cp in own:
+        cp.start()
+
     barrier = pltpu.get_barrier_semaphore()
     loop(Z, lambda k: pl.semaphore_signal(barrier, inc=1, device_id=zpeer(k), device_id_type=MESH), 1)
     loop(NPL, lambda k: pl.semaphore_signal(barrier, inc=1, device_id=plane(k), device_id_type=MESH), 1)
@@ -78,12 +100,9 @@
     y_up = dev(x, lax.rem(y + 1, NY), z, c)
     y_down = dev(x, lax.rem(y + NY - 1, NY), z, c)
 
-    def half(i):
-        return pl.ds(pl.multiple_of(i * H, H), H)
-
     pair_w = remote(w.at[:, half(1 - yl)], wbuf.at[z, yl, c], pair_s.at[0], pair_r.at[0], partner)
     pair_w.start()
-    wbuf[z, yl, c] = w[:, half(yl)]
+    own[0].wait()
 
     def at(direction, s):
         return lax.rem(z + (Z - s if direction == 0 else s), Z)
@@ -122,9 +141,6 @@
         sib(0, a, 0).start()
 
     first(yl)
-
-    b_mine, h_mine = lax.div(mp, 2), lax.rem(mp, 2)
-    qrows = pl.ds(pl.multiple_of(h_mine * 16, 16), 16)
 
     def quad_of(k):
         q = lax.rem(quarter + k, 4)
@@ -145,21 +161,24 @@
     for k in (1, 2, 3):
         for cp in quad(k):
             cp.start()
-    qi_raw[0] = qi[qrows, pl.ds(pl.multiple_of(quarter * (D // 4), 128), D // 4)]
-    qh_raw[0] = qh[:, pl.ds(pl.multiple_of(quarter * QC, 128), QC)]
-    pair_meta = remote(meta, meta2, pair_s.at[1], pair_r.at[1], partner)
-    pair_meta.start()
+    pair_routes = remote(routes, keys.at[2], pair_s.at[1], pair_r.at[1], partner)
+    pair_routes.start()
+    pair_slots = remote(slots, keys.at[3], pair_s.at[3], pair_r.at[3], partner)
+    pair_slots.start()
 
     pair_w.wait_recv()
     first(1 - yl)
+    own[4].wait()
     for s in (0, 1, 2):
         tok_start(0, s)
         tok_start(1, s)
-    pair_hg = remote(hg.at[:, half(1 - yl)], hg2, pair_s.at[2], pair_r.at[2], partner)
+    pair_hg = remote(hg_in.at[:, half(1 - yl)], hg2, pair_s.at[2], pair_r.at[2], partner)
 
     for k in (1, 2, 3):
         for cp in quad(k):
             cp.wait_recv()
+    for i in (1, 2, 3):
+        own[i].wait()
     srcs = []
     for k in range(4):
         q = lax.rem(quarter + 4 - k, 4)
@@ -298,18 +317,21 @@
     multiply(0, S)
 
     pair_hg.wait_recv()
-    pair_meta.wait_recv()
+    pair_routes.wait_recv()
+    pair_slots.wait_recv()
+    for i in (5, 6, 7, 8):
+        own[i].wait()
     fh_sib.wait_recv()
     fh_own = fbuf[:, :, 128:].reshape(NC * 16, QC)
     fh_other = fsib[...].reshape(NC * 16, QC)
     fh = jnp.concatenate([jnp.where(c == 0, fh_own, fh_other), jnp.where(c == 0, fh_other, fh_own)], axis=1)
-    shift = bias[:, half(yl)]
+    shift = bias[...]
     rows = 32
     for g in (0, 1):
 
         def some(i, carry, g=g):
             at_rows = pl.ds(pl.multiple_of(i * rows, rows), rows)
-            grads = hg[at_rows, half(yl)] if g == 0 else hg2[at_rows, :]
+            grads = hg[at_rows, :] if g == 0 else hg2[at_rows, :]
             delta = grads.astype(jnp.float32) * slope(acc[g, at_rows, :] + shift)
             high = delta.astype(jnp.bfloat16)
             dhi[g, at_rows, :] = high
@@ -319,18 +341,20 @@
         lax.fori_loop(0, T // rows, some, 0)
     loop(NPL // 2, lambda k: lf_arrived(k).wait_recv(), 1)
     total = jnp.zeros((Z * 4, 128), jnp.float32)
+    bits = Z.bit_length()
     n_q = NC * 16 // RANK
     for g in (0, 1):
         right = lax.dot_general(fh, dhi[g], NT, preferred_element_type=jnp.float32)
         right = right + lax.dot_general(fh, dlo[g], NT, preferred_element_type=jnp.float32)
         left = left_all[yl if g == 0 else 1 - yl].reshape(NC * 16, T)
         contrib = (left * right).reshape(n_q, RANK, T).sum(axis=1)
-        keys = meta[...] if g == 0 else meta2[...]
+        dest, slot = keys[2 * g], keys[2 * g + 1]
+        there = (dest >> 1 & Z - 1) * 4 + (dest >> bits) * 2 + (dest & 1)
         wide = jnp.concatenate([contrib] * (128 // n_q), axis=0)
         slot_of = lax.div(lax.broadcasted_iota(jnp.int32, (128, T), 0), n_q)
-        wide = jnp.where(slot_of == keys[1:2], wide, 0.0)
+        wide = jnp.where(slot_of == slot, wide, 0.0)
         place = lax.broadcasted_iota(jnp.int32, (Z * 4, T), 0)
-        named = jnp.where(place == keys[0:1], 1.0, 0.0).astype(jnp.bfloat16)
+        named = jnp.where(place == there, 1.0, 0.0).astype(jnp.bfloat16)
         high = wide.astype(jnp.bfloat16)
         rest = wide - high.astype(jnp.float32)
         mid = rest.astype(jnp.bfloat16)
@@ -362,9 +386,11 @@
 
     mine = lax.fori_loop(1, NPL, add2, mine)
     row = lax.broadcasted_iota(jnp.int32, (4, 128), 0)
-    out[...] = jnp.sum(jnp.where(row == quarter, mine, 0.0), axis=0, keepdims=True)
-
-    for cp in (pair_w, pair_meta, pair_hg, fh_sib):
+    scores = jnp.sum(jnp.where(row == quarter, mine, 0.0), axis=0, keepdims=True)
+    for e in range(EX_OUT):
+        out[e : e + 1, :] = scores[:, e * n_q : (e + 1) * n_q]
+
+    for cp in (pair_w, pair_routes, pair_slots, pair_hg, fh_sib):
         cp.wait_send()
     for direction in (0, 1):
         for a in (0, 1):
@@ -401,20 +427,22 @@
     NC = 2 * NB
     NY, S = 2 * YH, Z // 2
     NPL = X * NY * 2
-    dest = routes[:, 0]
-    place = lax.rem(lax.div(dest, 2), Z) * 4 + lax.div(dest, 2 * Z) * 2 + lax.rem(dest, 2)
-    meta = jnp.concatenate([place[None], example_slot[None], jnp.zeros((6, T), jnp.int32)])
     bf, f32 = jnp.bfloat16, jnp.float32
     dma = pltpu.SemaphoreType.DMA
     vmem = pl.BlockSpec(memory_space=pltpu.VMEM)
+    anywhere = pl.BlockSpec(memory_space=pl.ANY)
     scratch = [
+        pltpu.SMEM(owners.shape, jnp.int32),
+        pltpu.VMEM((T, D), bf),
+        pltpu.VMEM((T, H), bf),
+        pltpu.VMEM((1, H), f32),
+        pltpu.VMEM((4, 1, T), jnp.int32),
         pltpu.VMEM((Z, 2, 2, w_in.shape[0], H), bf),
         pltpu.VMEM((T, D), bf),
         pltpu.VMEM((2, T, H), f32),
         pltpu.VMEM((T, H), bf),
         pltpu.VMEM((2, T, H), bf),
         pltpu.VMEM((2, T, H), bf),
-        pltpu.VMEM((8, T), jnp.int32),
         pltpu.VMEM((4, 16, D // 4), bf),
         pltpu.VMEM((4, M, QC), bf),
         pltpu.VMEM((NC, 16, 128 + QC), bf),
@@ -429,21 +457,19 @@
         pltpu.VMEM((4, 128), f32),
         pltpu.VMEM((NPL, 4, 128), f32),
     ]
-    scratch += [dma((2, 2, S + 1))] * 4 + [dma((2, S + 1, 2))] * 2 + [dma((3,))] * 2
+    scratch += [dma((2, 2, S + 1))] * 4 + [dma((2, S + 1, 2))] * 2 + [dma((4,))] * 2
     scratch += [dma((2, 4))] * 2 + [dma((NC,)), dma((Z,)), dma((Z,)), dma((NC,))] + [dma((4,))] * 2
-    scratch += [dma((NPL // 2,))] * 2 + [dma((Z,))] * 2 + [dma((NPL,))] * 2 + [dma((1,))]
-    scores = pl.pallas_call(
+    scratch += [dma((NPL // 2,))] * 2 + [dma((Z,))] * 2 + [dma((NPL,))] * 2 + [dma((9,))]
+    return pl.pallas_call(
         functools.partial(kernel, X, YH, Z, NB),
-        out_shape=jax.ShapeDtypeStruct((1, 128), f32),
-        in_specs=[pl.BlockSpec(memory_space=pltpu.SMEM)] + [vmem] * 7,
+        out_shape=jax.ShapeDtypeStruct((EX_OUT, NC * 16 // RANK), f32),
+        in_specs=[anywhere] * 9,
         out_specs=vmem,
         scratch_shapes=scratch,
         compiler_params=pltpu.CompilerParams(
-            collective_id=0, has_side_effects=True, vmem_limit_bytes=48 * 2**20
+            collective_id=0, has_side_effects=True, vmem_limit_bytes=60 * 2**20
         ),
-    )(owners, tokens, hidden_grad, w_in, b_in[None], query_in, query_hidden, meta)
-    n_q = NC * 16 // RANK
-    return scores[:, : EX_OUT * n_q].reshape(EX_OUT, n_q)
+    )(owners, tokens, hidden_grad, w_in, b_in[None], query_in, query_hidden, routes.reshape(1, T), example_slot[None])
 
 
 def solution(mesh, YH=2):

time: 90.7 us -> 82 us (0.904)
  local copies, waits for them, and re-layouts: 7.93 us -> 1.28 us
  other arithmetic: 2.1 us -> 0 us
    unnamed x14 -> x1, local copies, waits for them, and re-layouts: 6.66 us -> 1.28 us
where the time goes in v3:
time: 82 us; the launch traced here: 81.8 us
  Pallas kernels  80.5 us (98%)
  local copies, waits for them, and re-layouts  1.28 us (2%)
    pallas_call x1, Pallas kernels, body(): pl.pallas_call(functools.partial(kernel, X, YH, Z, NB), out_shape=jax.Sha...  80.5 us

profile of v3, /device:TPU:1, one launch (start us, length us, event | category | flops | bytes accessed | tf_op | source)
XLA Modules:
  0.0 81.8 jit_solution(13309289128740803099)
XLA Ops:
  0.0 80.5 %shard_map.91 = f32[8,16]{1,0:T(8,128)} custom-call(s32[64]{0:T(128)} %owners_in.1, bf16[256,4096]{1,0:T(8,128)(2,1)} %tok_in.1, bf16[256,1024]{1,0:T(8,128)(2,1)} %hg_in.1, bf16[64,1024]{1,0:T(8,128)(2,1)} %w.1, f32[1,1024]{1,0:T(1,128)} %bitcast.3, bf16[32,4096]{1,0:T(8,128)(2,1)} %qi.1, bf16[32,1024]{1,0:T(8,128)(2,1)} %qh.1, s32[1,256]{1,0:T(1,128)} %bitcast.4, ...), custom_call_target="tpu_custom_call" | custom-call | tf_op jit(solution)/shard_map/pallas_call | solution.py:463
  80.5 1.3 %copy.11 = f32[8,16]{1,0:T(8,128)} copy(f32[8,16]{1,0:T(8,128)} %shard_map.91) | data formatting | bytes 1024

commit v4 on v2

--- a/solution.py
+++ b/solution.py
@@ -24,17 +24,16 @@
     owners_in, tok_in, hg_in, w, bias_in, qi, qh, routes, slots, out,
     owners, tokens, hg, bias, keys,
     wbuf, tok2, acc, hg2, dhi, dlo,
-    qi_raw, qh_raw, gbuf, rs_in, red, fbuf, fsib, fpair, left_all,
+    qi_raw, qh_raw, gbuf, st1, hbuf, st2, fbuf, fsib, fpair, left_all,
     terms, t1_in, psum, t2_in,
     ring_s, ring_r, sib_s, sib_r, tok_s, tok_r, pair_s, pair_r, quad_s, quad_r,
-    rs_s, rs_r, ag_s, ag_r, fq_s, fq_r, lf_s, lf_r, t1_s, t1_r, t2_s, t2_r, loc_s, know,
+    r1_s, r1_r, r2_s, r2_r, aa_s, aa_r, ab_s, ab_r, fq_s, fq_r, lf_s, lf_r, t1_s, t1_r, t2_s, t2_r, loc_s,
 ):
     NY, S, NC = 2 * YH, Z // 2, 2 * NB
     T, D = tok_in.shape
     WR, H = w.shape[0], w.shape[1] // 2
     QC = H // 2
     NPL = X * NY * 2
-    R = Z // NC
     dp, mp = lax.axis_index("dp"), lax.axis_index("mp")
     c = lax.rem(dp, 2)
     z = lax.rem(lax.div(dp, 2), Z)
@@ -89,25 +88,10 @@
     for cp in own:
         cp.start()
 
-    def steps(n, k):
-        return sorted({k % n, -k % n} - {0}) if k < n else []
-
-    def circle(kx, ky, kz, core):
-        found = [dev(lax.rem(x + k, X), y, z, c) for k in (steps(X, kx) if kx else [])]
-        found += [dev(x, lax.rem(y + k, NY), z, c) for k in (steps(NY, ky) if ky else [])]
-        found += [zpeer(k) for k in (steps(Z, kz) if kz else [])]
-        return found + ([dev(x, y, z, 1 - c)] if core else [])
-
-    def tell(sem, devices):
-        for to in devices:
-            pl.semaphore_signal(sem, inc=1, device_id=to, device_id_type=MESH)
-
-    near = circle(1, 1, 1, True)
-    far2 = circle(2, 2, 2, True)
-    far4 = circle(0, 0, 4, True)
     barrier = pltpu.get_barrier_semaphore()
-    tell(barrier, near)
-    pl.semaphore_wait(barrier, len(near))
+    loop(Z, lambda k: pl.semaphore_signal(barrier, inc=1, device_id=zpeer(k), device_id_type=MESH), 1)
+    loop(NPL, lambda k: pl.semaphore_signal(barrier, inc=1, device_id=plane(k), device_id_type=MESH), 1)
+    pl.semaphore_wait(barrier, Z - 1 + NPL - 1)
 
     sibling = dev(x, y, z, 1 - c)
     partner = dev(x, yh * 2 + 1 - yl, z, c)
@@ -156,7 +140,6 @@
         sib(0, a, 0).start()
 
     first(yl)
-    tell(know.at[0], near)
 
     def quad_of(k):
         q = lax.rem(quarter + k, 4)
@@ -174,6 +157,9 @@
         )
         return a, b
 
+    for k in (1, 2, 3):
+        for cp in quad(k):
+            cp.start()
     pair_routes = remote(routes, keys.at[2], pair_s.at[1], pair_r.at[1], partner)
     pair_routes.start()
     pair_slots = remote(slots, keys.at[3], pair_s.at[3], pair_r.at[3], partner)
@@ -187,11 +173,6 @@
         tok_start(1, s)
     pair_hg = remote(hg_in.at[:, half(1 - yl)], hg2, pair_s.at[2], pair_r.at[2], partner)
 
-    pl.semaphore_wait(know.at[0], len(near))
-    for k in (1, 2, 3):
-        for cp in quad(k):
-            cp.start()
-    tell(know.at[1], far2)
 
     def pick_factors():
         for k in (1, 2, 3):
@@ -211,53 +192,113 @@
             b, h = i // 2, i % 2
             gi = sum(pick(b_mine, k) * qi_raw[k, :, i * 128 : (i + 1) * 128].astype(jnp.float32) for k in range(4))
             gh = sum(pick(b, k) * qh_raw[k, h * 16 : (h + 1) * 16].astype(jnp.float32) for k in range(4))
-            gbuf[i, :, :128] = gi.astype(jnp.bfloat16)
-            gbuf[i, :, 128:] = gh.astype(jnp.bfloat16)
-
-    is_red = lax.rem(z, R) == 0
-    my_chunk = lax.div(z, R)
-
-    def rs(i):
-        k = lax.rem(z + Z - i * R, Z)
-        return remote(gbuf.at[i], rs_in.at[k], rs_s.at[i], rs_r.at[k], dev(x, y, i * R, c))
-
-    def rs_arrived(k):
-        return remote(gbuf.at[0], rs_in.at[k], rs_s.at[0], rs_r.at[k], up)
-
-    def ag(k):
-        return remote(red, fbuf.at[my_chunk], ag_s.at[k], ag_r.at[my_chunk], zpeer(k))
-
-    def ag_arrived(i):
-        return remote(red, fbuf.at[i], ag_s.at[0], ag_r.at[i], up)
-
-    def not_mine(f):
-        def go(i):
-            @pl.when(i * R != z)
-            def _():
-                f(i)
-
-        return go
-
-    def reduce_factors():
-        @pl.when(is_red)
-        def _():
-            def add(k, total):
-                rs_arrived(k).wait_recv()
-                return total + rs_in[k].astype(jnp.float32)
-
-            total = lax.fori_loop(1, Z, add, gbuf[my_chunk].astype(jnp.float32))
-            red[...] = total.astype(jnp.bfloat16)
-            fbuf[my_chunk] = total.astype(jnp.bfloat16)
-            loop(Z, lambda k: ag(k).start(), 1)
+            gbuf[i % 2, i // 2, :, :128] = gi.astype(jnp.bfloat16)
+            gbuf[i % 2, i // 2, :, 128:] = gh.astype(jnp.bfloat16)
+
+    NH = Z // 4
+    even = lax.rem(z, 2) == 0
+    group, u0 = lax.rem(lax.div(z, 2), 2), lax.div(z, 4)
+
+    def to_head(n):
+        src = gbuf.at[group if n == 0 else 1 - group]
+        return remote(src, st1.at[n], r1_s.at[n], r1_r.at[n], zpeer((Z - 1, Z - 2, 1)[n]))
+
+    def between_heads(m):
+        return remote(hbuf.at[lax.rem(u0 + m, NH)], st2.at[m], r2_s.at[m], r2_r.at[m], zpeer(4 * m))
+
+    def share(m):
+        ref = fbuf.at[group, u0]
+        return remote(ref, ref, aa_s.at[m], aa_r.at[m], zpeer(4 * m))
+
+    def share_arrived(m):
+        ref = fbuf.at[group, lax.rem(u0 + NH - m, NH)]
+        return remote(ref, ref, aa_s.at[m], aa_r.at[m], up)
+
+    def from_head(n):
+        ref = fbuf.at[group]
+        return remote(ref, ref, ab_s.at[n], ab_r.at[n], zpeer((Z - 1, Z - 2, 1)[n]))
+
+    def head_arrived(n):
+        ref = fbuf.at[group if n == 2 else 1 - group]
+        return remote(ref, ref, ab_s.at[n], ab_r.at[n], up)
+
+    def when_even(f):
+        pl.when(even)(f)
+
+    def when_odd(f):
+        pl.when(jnp.logical_not(even))(f)
+
+    def stage1():
+        @when_odd
+        def _():
+            to_head(0).start()
+            to_head(2).start()
+
+        @when_even
+        def _():
+            to_head(1).start()
+
+    def stage2():
+        @when_even
+        def _():
+            total = gbuf[group].astype(jnp.float32)
+            for n in range(3):
+                to_head(n).wait_recv()
+                total = total + st1[n].astype(jnp.float32)
+            hbuf[...] = total.astype(jnp.bfloat16)
+            for m in range(1, NH):
+                between_heads(m).start()
+
+    def stage3():
+        @when_even
+        def _():
+            total = hbuf[u0].astype(jnp.float32)
+            for m in range(1, NH):
+                between_heads(m).wait_recv()
+                total = total + st2[m].astype(jnp.float32)
+            fbuf[group, u0] = total.astype(jnp.bfloat16)
+            for m in range(1, NH):
+                share(m).start()
+
+    def stage4():
+        @when_even
+        def _():
+            for m in range(1, NH):
+                share_arrived(m).wait_recv()
+            for n in range(3):
+                from_head(n).start()
+
+    def stages_sent():
+        @when_odd
+        def _():
+            to_head(0).wait_send()
+            to_head(2).wait_send()
+
+        @when_even
+        def _():
+            to_head(1).wait_send()
+            for m in range(1, NH):
+                between_heads(m).wait_send()
+                share(m).wait_send()
+            for n in range(3):
+                from_head(n).wait_send()
 
     def fq(k):
         _, to = quad_of(k)
-        return remote(fbuf.at[:, :, pl.ds(0, 128)], fpair.at[k - 1], fq_s.at[k], fq_r.at[k], to)
-
-    fh_sib = remote(fbuf.at[:, :, pl.ds(128, QC)], fsib, fq_s.at[0], fq_r.at[0], sibling)
+        return remote(fbuf.at[:, :, :, pl.ds(0, 128)], fpair.at[k - 1], fq_s.at[k], fq_r.at[k], to)
+
+    fh_sib = remote(fbuf.at[:, :, :, pl.ds(128, QC)], fsib, fq_s.at[0], fq_r.at[0], sibling)
 
     def gather_factors():
-        loop(NC, not_mine(lambda i: ag_arrived(i).wait_recv()))
+        @when_odd
+        def _():
+            head_arrived(0).wait_recv()
+            head_arrived(2).wait_recv()
+
+        @when_even
+        def _():
+            head_arrived(1).wait_recv()
+
         fh_sib.start()
         for k in (1, 2, 3):
             fq(k).start()
@@ -281,10 +322,9 @@
             q = lax.rem(quarter + 4 - k, 4)
             if k:
                 fq(k).wait_recv()
-            for i in range(NC):
-                f = fbuf[i, :, :128] if k == 0 else fpair[k - 1, i]
-                kk = pl.ds(pl.multiple_of(q * (D // 4) + i * 128, 128), 128)
-                total = total + lax.dot_general(f, tokens[:, kk], NT, preferred_element_type=jnp.float32)
+            f = jnp.concatenate([fbuf[i % 2, i // 2, :, :128] if k == 0 else fpair[k - 1, i % 2, i // 2] for i in range(NC)], axis=1)
+            kk = pl.ds(pl.multiple_of(q * (D // 4), D // 4), D // 4)
+            total = total + lax.dot_general(f, tokens[:, kk], NT, preferred_element_type=jnp.float32)
         left_all[yl, mp] = total
         loop(NPL // 2, lambda k: lf(k).start(), 1)
 
@@ -312,6 +352,8 @@
                 ring(direction, a, s + 1).start()
             sib(direction, a, s).start()
 
+    pick_factors()
+    stage1()
     acc[...] = jnp.zeros_like(acc)
     for s in range(1, S + 1):
         for direction, a in ((0, 0), (1, 1), (0, 1), (1, 0)):
@@ -320,15 +362,17 @@
             tok_start(0, s + 2)
             tok_start(1, s + 2)
         if s == 1:
-            pl.semaphore_wait(know.at[1], len(far2))
-            tell(know.at[2], far4)
-            pick_factors()
+            stage2()
         if s == min(2, S):
-            pl.semaphore_wait(know.at[2], len(far4))
-            loop(NC, not_mine(lambda i: rs(i).start()))
             pair_hg.start()
+        if s == min(3, S):
+            stage3()
+        if s == min(4, S):
+            stage4()
         if s == min(5, S):
-            reduce_factors()
+            gather_factors()
+        if s == min(6, S):
+            left_part()
         if s == 2:
             multiply(1, 0)
         elif s > 2:
@@ -339,8 +383,6 @@
     else:
         multiply(0, S - 1)
         multiply(1, S - 1)
-    gather_factors()
-    left_part()
     multiply(0, S)
 
     pair_hg.wait_recv()
@@ -349,8 +391,8 @@
     for i in (5, 6, 7, 8):
         own[i].wait()
     fh_sib.wait_recv()
-    fh_own = fbuf[:, :, 128:].reshape(NC * 16, QC)
-    fh_other = fsib[...].reshape(NC * 16, QC)
+    fh_own = jnp.concatenate([fbuf[i % 2, i // 2, :, 128:] for i in range(NC)], axis=0)
+    fh_other = jnp.concatenate([fsib[i % 2, i // 2] for i in range(NC)], axis=0)
     fh = jnp.concatenate([jnp.where(c == 0, fh_own, fh_other), jnp.where(c == 0, fh_other, fh_own)], axis=1)
     shift = bias[...]
     rows = 32
@@ -434,11 +476,7 @@
         for cp in quad(k):
             cp.wait_send()
         fq(k).wait_send()
-    loop(NC, not_mine(lambda i: rs(i).wait_send()))
-
-    @pl.when(is_red)
-    def _():
-        loop(Z, lambda k: ag(k).wait_send(), 1)
+    stages_sent()
 
     loop(NPL // 2, lambda k: lf(k).wait_send(), 1)
     loop(Z, lambda k: t1(k).wait_send(), 1)
@@ -454,6 +492,7 @@
     NC = 2 * NB
     NY, S = 2 * YH, Z // 2
     NPL = X * NY * 2
+    NH = Z // 4
     bf, f32 = jnp.bfloat16, jnp.float32
     dma = pltpu.SemaphoreType.DMA
     vmem = pl.BlockSpec(memory_space=pltpu.VMEM)
@@ -472,12 +511,13 @@
         pltpu.VMEM((2, T, H), bf),
         pltpu.VMEM((4, 16, D // 4), bf),
         pltpu.VMEM((4, M, QC), bf),
-        pltpu.VMEM((NC, 16, 128 + QC), bf),
-        pltpu.VMEM((Z, 16, 128 + QC), bf),
-        pltpu.VMEM((16, 128 + QC), bf),
-        pltpu.VMEM((NC, 16, 128 + QC), bf),
-        pltpu.VMEM((NC, 16, QC), bf),
-        pltpu.VMEM((3, NC, 16, 128), bf),
+        pltpu.VMEM((2, NH, 16, 128 + QC), bf),
+        pltpu.VMEM((3, NH, 16, 128 + QC), bf),
+        pltpu.VMEM((NH, 16, 128 + QC), bf),
+        pltpu.VMEM((NH, 16, 128 + QC), bf),
+        pltpu.VMEM((2, NH, 16, 128 + QC), bf),
+        pltpu.VMEM((2, NH, 16, QC), bf),
+        pltpu.VMEM((3, 2, NH, 16, 128), bf),
         pltpu.VMEM((2, X * YH, 16, T), f32),
         pltpu.VMEM((Z, 4, 128), f32),
         pltpu.VMEM((Z, 4, 128), f32),
@@ -485,8 +525,8 @@
         pltpu.VMEM((NPL, 4, 128), f32),
     ]
     scratch += [dma((2, 2, S + 1))] * 4 + [dma((2, S + 1, 2))] * 2 + [dma((4,))] * 2
-    scratch += [dma((2, 4))] * 2 + [dma((NC,)), dma((Z,)), dma((Z,)), dma((NC,))] + [dma((4,))] * 2
-    scratch += [dma((NPL // 2,))] * 2 + [dma((Z,))] * 2 + [dma((NPL,))] * 2 + [dma((9,)), pltpu.SemaphoreType.REGULAR((3,))]
+    scratch += [dma((2, 4))] * 2 + ([dma((3,))] * 2 + [dma((NH,))] * 4 + [dma((3,))] * 2) + [dma((4,))] * 2
+    scratch += [dma((NPL // 2,))] * 2 + [dma((Z,))] * 2 + [dma((NPL,))] * 2 + [dma((9,))]
     return pl.pallas_call(
         functools.partial(kernel, X, YH, Z, NB),
         out_shape=jax.ShapeDtypeStruct((EX_OUT, NC * 16 // RANK), f32),

time: 91.4 us -> 79.9 us (0.87)
  Pallas kernels: 90 us -> 78.5 us
    pallas_call x1, Pallas kernels: 90 us -> 78.5 us  [body(): pl.pallas_call(functools.partial(kernel, X, YH, Z, NB), out_shape=jax.Sha...]
where the time goes in v4:
time: 79.9 us; the launch traced here: 79.8 us
  Pallas kernels  78.5 us (98%)
  local copies, waits for them, and re-layouts  1.28 us (2%)
    pallas_call x1, Pallas kernels, body(): pl.pallas_call(functools.partial(kernel, X, YH, Z, NB), out_shape=jax.Sha...  78.5 us

profile of v4, /device:TPU:1, one launch (start us, length us, event | category | flops | bytes accessed | tf_op | source)
XLA Modules:
  0.0 79.8 jit_solution(14117729769228588914)
XLA Ops:
  0.0 78.5 %shard_map.91 = f32[8,16]{1,0:T(8,128)} custom-call(s32[64]{0:T(128)} %owners_in.1, bf16[256,4096]{1,0:T(8,128)(2,1)} %tok_in.1, bf16[256,1024]{1,0:T(8,128)(2,1)} %hg_in.1, bf16[64,1024]{1,0:T(8,128)(2,1)} %w.1, f32[1,1024]{1,0:T(1,128)} %bitcast.3, bf16[32,4096]{1,0:T(8,128)(2,1)} %qi.1, bf16[32,1024]{1,0:T(8,128)(2,1)} %qh.1, s32[1,256]{1,0:T(1,128)} %bitcast.4, ...), custom_call_target="tpu_custom_call" | custom-call | tf_op jit(solution)/shard_map/pallas_call | solution.py:530
  78.5 1.3 %copy.11 = f32[8,16]{1,0:T(8,128)} copy(f32[8,16]{1,0:T(8,128)} %shard_map.91) | data formatting | bytes 1024

commit v5 on v4

--- a/solution.py
+++ b/solution.py
@@ -356,6 +356,12 @@
     stage1()
     acc[...] = jnp.zeros_like(acc)
     for s in range(1, S + 1):
+        if s == S:
+            for t in (S - 2, S - 1):
+                if t > 0:
+                    multiply(0, t)
+                if t >= 0:
+                    multiply(1, t)
         for direction, a in ((0, 0), (1, 1), (0, 1), (1, 0)):
             advance(direction, a, s)
         if s + 2 <= S:
@@ -373,16 +379,10 @@
             gather_factors()
         if s == min(6, S):
             left_part()
-        if s == 2:
-            multiply(1, 0)
-        elif s > 2:
-            multiply(0, s - 2)
+        if 2 <= s < S:
+            if s > 2:
+                multiply(0, s - 2)
             multiply(1, s - 2)
-    if S == 1:
-        multiply(1, 0)
-    else:
-        multiply(0, S - 1)
-        multiply(1, S - 1)
     multiply(0, S)
 
     pair_hg.wait_recv()
@@ -439,7 +439,13 @@
     def t2(k):
         return remote(psum, t2_in.at[k], t2_s.at[k], t2_r.at[k], plane(k))
 
-    loop(Z, lambda k: t1(k).start(), 1)
+    t1(S).start()
+
+    def farthest_first(i):
+        t1(S + i).start()
+        t1(S - i).start()
+
+    loop(S, farthest_first, 1)
 
     def add1(k, total):
         t1(k).wait_recv()

time: 79.9 us -> 79.3 us (level)
  no operation moved by 1% of the time
where the time goes in v5:
time: 79.3 us; the launch traced here: 79.2 us
  Pallas kernels  77.9 us (98%)
  local copies, waits for them, and re-layouts  1.28 us (2%)
    pallas_call x1, Pallas kernels, body(): pl.pallas_call(functools.partial(kernel, X, YH, Z, NB), out_shape=jax.Sha...  77.9 us

profile of v5, /device:TPU:1, one launch (start us, length us, event | category | flops | bytes accessed | tf_op | source)
XLA Modules:
  0.0 79.2 jit_solution(12813989034461671539)
XLA Ops:
  0.0 77.9 %shard_map.91 = f32[8,16]{1,0:T(8,128)} custom-call(s32[64]{0:T(128)} %owners_in.1, bf16[256,4096]{1,0:T(8,128)(2,1)} %tok_in.1, bf16[256,1024]{1,0:T(8,128)(2,1)} %hg_in.1, bf16[64,1024]{1,0:T(8,128)(2,1)} %w.1, f32[1,1024]{1,0:T(1,128)} %bitcast.3, bf16[32,4096]{1,0:T(8,128)(2,1)} %qi.1, bf16[32,1024]{1,0:T(8,128)(2,1)} %qh.1, s32[1,256]{1,0:T(1,128)} %bitcast.4, ...), custom_call_target="tpu_custom_call" | custom-call | tf_op jit(solution)/shard_map/pallas_call | solution.py:536
  77.9 1.3 %copy.11 = f32[8,16]{1,0:T(8,128)} copy(f32[8,16]{1,0:T(8,128)} %shard_map.91) | data formatting | bytes 1024
